TPU v7x, 256 devices: a whole 4x4x8 slice. The times are simulated.
256 devices in a mesh: seq: 32 (over z_hi, y, core), tp: 8 (over z_lo, x).
Axes of the slice: x: 4, y: 4, z: 8 (z_hi: 4, z_lo: 2; z = z_hi * 2 + z_lo), core: 2. Of those that a mesh axis runs over, the one named last changes fastest.
Arguments:
- sol_q: bfloat16 [8192, 5120], P('seq', 'tp')
- solution_keys: bfloat16 [8192, 1024], P('seq', 'tp')
- solution_values: bfloat16 [8192, 1024], P('seq', 'tp'), may hold values from -6 to 6
- crit_q: bfloat16 [64, 256, 5120], P('seq', None, 'tp')
- crit_k: bfloat16 [64, 256, 1024], P('seq', None, 'tp')
- critique_values: bfloat16 [64, 256, 1024], P('seq', None, 'tp'), may hold values from -6 to 6
- boundary: int32 [64], replicated, may hold values from 1 to 8192, as said below
- w_out: bfloat16 [5120, 5120], P('tp'), may hold values from -0.078125 to 0.078125
Outputs:
- sol_out: bfloat16 [8192, 5120], P('seq', 'tp')
- crit_out: bfloat16 [64, 256, 5120], P('seq', None, 'tp')
Inputs may be any that keep to these rules, and one draw needn't show every extreme that they name: Strictly increasing over critiques; boundary[c] lies between c * 128 + 1 and (c + 1) * 128; the last one equals 8192.
All inputs are finite; a program needn't handle non-finite values.
Results may differ from a plain program's by a relative error of at most 0.02.
Values may be sent and summed in bfloat16 or wider, within the bound.
A program may use at most 128 MiB of HBM per device.

v0:
```python
import math

import jax
import jax.numpy as jnp
from jax import lax
from jax.sharding import PartitionSpec as P

HEAD_WIDTH = 128


NEG = -1e30


def absorb(running, scores, value_list, spec):
    top_score, weight_sum, numerator = running
    new_top = jnp.maximum(top_score, jnp.max(scores, axis=-1))
    rescale = jnp.exp(top_score - new_top)
    weights = jnp.exp(scores - new_top[..., None])
    weight_sum = weight_sum * rescale + jnp.sum(weights, axis=-1)
    numerator = numerator * rescale[..., None] + jnp.einsum(
        spec, weights.astype(jnp.bfloat16), value_list, preferred_element_type=jnp.float32
    )
    return (new_top, weight_sum, numerator)


def over_blocks(carry, pieces, kv_heads, update):
    key_list, value_list = pieces
    key_rows = key_list.shape[0]
    block_rows = math.gcd(key_rows, 512)
    block_count = key_rows // block_rows
    key_blocks = key_list.reshape(block_count, block_rows, kv_heads, HEAD_WIDTH)
    value_blocks = value_list.reshape(block_count, block_rows, kv_heads, HEAD_WIDTH)

    def advance(running, members):
        key_block, value_block, block_offset = members
        return (update(running, key_block, value_block, block_offset * block_rows), None)

    carry, _ = lax.scan(
        advance, carry, (key_blocks, value_blocks, jnp.arange(block_count, dtype=jnp.int32))
    )
    return carry


def finish(running):
    return running[2] / running[1][..., None]


def per_device(
    sol_q, solution_keys, solution_values, crit_q, crit_k, critique_values, boundary, w_out
):
    kv_heads = solution_keys.shape[1] // HEAD_WIDTH
    group_length = sol_q.shape[1] // solution_keys.shape[1]
    sol_rows = sol_q.shape[0]
    critiques = crit_q.shape[0]
    crit_len = crit_q.shape[1]
    score_scale = HEAD_WIDTH ** (-0.5)
    device_index = lax.axis_index("seq")
    slots = jnp.arange(critiques, dtype=jnp.int32)
    critique_ids = device_index * critiques + slots
    limits = jnp.take(boundary, critique_ids)
    deepest = jnp.max(limits)
    query_pos = device_index * sol_rows + jnp.arange(sol_rows, dtype=jnp.int32)
    last_query = jnp.max(query_pos)
    sol_queries = sol_q.reshape(sol_rows, kv_heads, group_length, HEAD_WIDTH)
    crit_queries = crit_q.reshape(critiques, crit_len, kv_heads, group_length, HEAD_WIDTH)
    self_key_rows = crit_k.reshape(critiques, crit_len, kv_heads, HEAD_WIDTH)
    self_value_rows = critique_values.reshape(critiques, crit_len, kv_heads, HEAD_WIDTH)
    self_scores = (
        jnp.einsum(
            "clngd,cknd->ngclk", crit_queries, self_key_rows, preferred_element_type=jnp.float32
        )
        * score_scale
    )
    causal = jnp.arange(crit_len)[None, :] <= jnp.arange(crit_len)[:, None]
    self_scores = jnp.where(causal, self_scores, NEG)
    self_top = jnp.max(self_scores, axis=-1)
    self_weights = jnp.exp(self_scores - self_top[..., None])
    crit_start = (
        self_top,
        jnp.sum(self_weights, axis=-1),
        jnp.einsum(
            "ngclk,cknd->ngcld",
            self_weights.astype(jnp.bfloat16),
            self_value_rows,
            preferred_element_type=jnp.float32,
        ),
    )
    sol_start = (
        jnp.full((kv_heads, group_length, sol_rows), NEG, jnp.float32),
        jnp.zeros((kv_heads, group_length, sol_rows), jnp.float32),
        jnp.zeros((kv_heads, group_length, sol_rows, HEAD_WIDTH), jnp.float32),
    )

    def solution_update(running, key_list, value_list, first_key):
        key_pos = first_key + jnp.arange(key_list.shape[0], dtype=jnp.int32)

        def solution_attend(current):
            scores = (
                jnp.einsum(
                    "rngd,knd->ngrk", sol_queries, key_list, preferred_element_type=jnp.float32
                )
                * score_scale
            )
            allowed = key_pos[None, :] <= query_pos[:, None]
            return absorb(current, jnp.where(allowed, scores, NEG), value_list, "ngrk,knd->ngrd")

        return lax.cond(first_key <= last_query, solution_attend, lambda current: current, running)

    def critique_update(running, key_list, value_list, first_key):
        key_pos = first_key + jnp.arange(key_list.shape[0], dtype=jnp.int32)

        def critique_attend(current):
            scores = (
                jnp.einsum(
                    "clngd,knd->ngclk", crit_queries, key_list, preferred_element_type=jnp.float32
                )
                * score_scale
            )
            allowed = key_pos[None, :] < limits[:, None]
            return absorb(
                current, jnp.where(allowed[:, None, :], scores, NEG), value_list, "ngclk,knd->ngcld"
            )

        return lax.cond(first_key < deepest, critique_attend, lambda current: current, running)

    sol_done = over_blocks(
        sol_start,
        (
            lax.all_gather(solution_keys, "seq", axis=0, tiled=True),
            lax.all_gather(solution_values, "seq", axis=0, tiled=True),
        ),
        kv_heads,
        solution_update,
    )
    crit_done = over_blocks(
        crit_start,
        (
            lax.all_gather(solution_keys, "seq", axis=0, tiled=True),
            lax.all_gather(solution_values, "seq", axis=0, tiled=True),
        ),
        kv_heads,
        critique_update,
    )
    sol_attention = (
        finish(sol_done).transpose(2, 0, 1, 3).reshape(sol_rows, -1).astype(jnp.bfloat16)
    )
    crit_attention = finish(crit_done).transpose(2, 3, 0, 1, 4).reshape(critiques, crit_len, -1)
    crit_attention = crit_attention.astype(jnp.bfloat16)
    joined = jnp.concatenate(
        [sol_attention, crit_attention.reshape(critiques * crit_len, -1)], axis=0
    )
    partial_out = jnp.dot(joined, w_out, preferred_element_type=jnp.float32)
    summed = lax.psum_scatter(
        partial_out.astype(jnp.bfloat16), "tp", scatter_dimension=1, tiled=True
    )
    return (summed[:sol_rows], summed[sol_rows:].reshape(critiques, crit_len, -1))


def solution(mesh):
    in_specs = (
        P("seq", "tp"),
        P("seq", "tp"),
        P("seq", "tp"),
        P("seq", None, "tp"),
        P("seq", None, "tp"),
        P("seq", None, "tp"),
        P(),
        P("tp", None),
    )
    out_specs = (P("seq", "tp"), P("seq", None, "tp"))
    return jax.shard_map(
        per_device, mesh=mesh, in_specs=in_specs, out_specs=out_specs, check_vma=False
    )
```

profile of v0, /device:TPU:216, one launch (start us, length us, event | category | flops | bytes accessed | tf_op | source)
XLA Modules:
  0.0 464.8 jit_solution(5356749955828790947)
XLA Ops:
  18.1 45.1 %all-gather.3.cloned.1.call-done = bf16[8192,128]{1,0:T(8,128)(2,1)} async-done(((bf16[256,128]{1,0:T(8,128)(2,1)}), bf16[8192,128]{1,0:T(8,128)(2,1)}) %all-gather.3.cloned.1.call-update) | async-done | bytes 2097168 | tf_op jit(solution)/shard_map/all_gather | solution.py:129
  63.2 54.3 %all-gather.5.cloned.1.call-done = bf16[8192,128]{1,0:T(8,128)(2,1)} async-done(((bf16[256,128]{1,0:T(8,128)(2,1)}), bf16[8192,128]{1,0:T(8,128)(2,1)}) %all-gather.5.cloned.1.call-update) | async-done | bytes 2097168 | tf_op jit(solution)/shard_map/all_gather | solution.py:130
  117.5 97.5 %while.30 = (s32[]{:T(128)}, f32[1,5,256]{2,1,0:T(8,128)S(1)}, f32[1,5,256]{2,1,0:T(8,128)S(1)}, f32[1,5,256,128]{3,2,1,0:T(8,128)S(1)}, s32[16]{0:T(128)S(1)}, ...) while((s32[]{:T(128)}, f32[1,5,256]{2,1,0:T(8,128)S(1)}, ...), condition=%wide.region_6.7_spmd.clone, body=%wide.region_1.6_spmd.clone.sunk | while | flops 343216640 | bytes 10384699 | solution.py:38
  131.8 4.2 conditional.6
  137.8 4.2 conditional.6
  143.9 4.2 conditional.6
  150.0 4.2 conditional.6
  156.1 4.2 conditional.6
  162.2 4.2 conditional.6
  168.2 4.2 conditional.6
  174.3 4.2 conditional.6
  180.4 4.2 conditional.6
  215.2 126.2 %while.29 = (s32[]{:T(128)}, f32[1,5,2,256]{3,1,2,0:T(8,128)S(1)}, f32[1,5,2,256]{3,1,2,0:T(8,128)S(1)}, f32[1,5,2,256,128]{4,3,2,1,0:T(8,128)S(1)}, s32[16]{0:T...) while((s32[]{:T(128)}, f32[1,5,2,256]{3,1,2,0:T(8,128)S(1)}, ...), condition=%wide.region_15.16_spmd, body=%wide.region_10.15_spmd.sunk | while | flops 682238976 | bytes 19454264 | solution.py:38
  217.1 6.0 %conditional.5 = ((f32[1,5,2,256]{3,1,2,0:T(8,128)S(1)}, f32[1,5,2,256]{3,1,2,0:T(8,128)S(1)}, f32[1,5,2,256,128]{4,3,2,1,0:T(8,128)S(1)})) conditional(s32[]{:T(128)} %convert_element_type.72, (f32[1,5,2,256]{3,1,2,0:T(8,128)S(1)}, f32[1,5,2,256]{3,1,2,0:T(8,128)S(1)}, f32[1,5,2,256,128]{4,3,2,1,0:T(8,128)S(1)}) %tuple.77, (s32[]{:T(128)}, ...), branch_computations={%region_11.11_spmd, %region_12.14_spmd} | conditional | flops 682238976 | bytes 19451948 | solution.py:124
  225.0 6.0 %conditional.5 = ((f32[1,5,2,256]{3,1,2,0:T(8,128)S(1)}, f32[1,5,2,256]{3,1,2,0:T(8,128)S(1)}, f32[1,5,2,256,128]{4,3,2,1,0:T(8,128)S(1)})) conditional(s32[]{:T(128)} %convert_element_type.72, (f32[1,5,2,256]{3,1,2,0:T(8,128)S(1)}, f32[1,5,2,256]{3,1,2,0:T(8,128)S(1)}, f32[1,5,2,256,128]{4,3,2,1,0:T(8,128)S(1)}) %tuple.77, (s32[]{:T(128)}, ...), branch_computations={%region_11.11_spmd, %region_12.14_spmd} | conditional | flops 682238976 | bytes 19451948 | solution.py:124
  232.9 6.0 %conditional.5 = ((f32[1,5,2,256]{3,1,2,0:T(8,128)S(1)}, f32[1,5,2,256]{3,1,2,0:T(8,128)S(1)}, f32[1,5,2,256,128]{4,3,2,1,0:T(8,128)S(1)})) conditional(s32[]{:T(128)} %convert_element_type.72, (f32[1,5,2,256]{3,1,2,0:T(8,128)S(1)}, f32[1,5,2,256]{3,1,2,0:T(8,128)S(1)}, f32[1,5,2,256,128]{4,3,2,1,0:T(8,128)S(1)}) %tuple.77, (s32[]{:T(128)}, ...), branch_computations={%region_11.11_spmd, %region_12.14_spmd} | conditional | flops 682238976 | bytes 19451948 | solution.py:124
  240.8 6.0 %conditional.5 = ((f32[1,5,2,256]{3,1,2,0:T(8,128)S(1)}, f32[1,5,2,256]{3,1,2,0:T(8,128)S(1)}, f32[1,5,2,256,128]{4,3,2,1,0:T(8,128)S(1)})) conditional(s32[]{:T(128)} %convert_element_type.72, (f32[1,5,2,256]{3,1,2,0:T(8,128)S(1)}, f32[1,5,2,256]{3,1,2,0:T(8,128)S(1)}, f32[1,5,2,256,128]{4,3,2,1,0:T(8,128)S(1)}) %tuple.77, (s32[]{:T(128)}, ...), branch_computations={%region_11.11_spmd, %region_12.14_spmd} | conditional | flops 682238976 | bytes 19451948 | solution.py:124
  248.7 6.0 %conditional.5 = ((f32[1,5,2,256]{3,1,2,0:T(8,128)S(1)}, f32[1,5,2,256]{3,1,2,0:T(8,128)S(1)}, f32[1,5,2,256,128]{4,3,2,1,0:T(8,128)S(1)})) conditional(s32[]{:T(128)} %convert_element_type.72, (f32[1,5,2,256]{3,1,2,0:T(8,128)S(1)}, f32[1,5,2,256]{3,1,2,0:T(8,128)S(1)}, f32[1,5,2,256,128]{4,3,2,1,0:T(8,128)S(1)}) %tuple.77, (s32[]{:T(128)}, ...), branch_computations={%region_11.11_spmd, %region_12.14_spmd} | conditional | flops 682238976 | bytes 19451948 | solution.py:124
  256.6 6.0 %conditional.5 = ((f32[1,5,2,256]{3,1,2,0:T(8,128)S(1)}, f32[1,5,2,256]{3,1,2,0:T(8,128)S(1)}, f32[1,5,2,256,128]{4,3,2,1,0:T(8,128)S(1)})) conditional(s32[]{:T(128)} %convert_element_type.72, (f32[1,5,2,256]{3,1,2,0:T(8,128)S(1)}, f32[1,5,2,256]{3,1,2,0:T(8,128)S(1)}, f32[1,5,2,256,128]{4,3,2,1,0:T(8,128)S(1)}) %tuple.77, (s32[]{:T(128)}, ...), branch_computations={%region_11.11_spmd, %region_12.14_spmd} | conditional | flops 682238976 | bytes 19451948 | solution.py:124
  264.5 6.0 %conditional.5 = ((f32[1,5,2,256]{3,1,2,0:T(8,128)S(1)}, f32[1,5,2,256]{3,1,2,0:T(8,128)S(1)}, f32[1,5,2,256,128]{4,3,2,1,0:T(8,128)S(1)})) conditional(s32[]{:T(128)} %convert_element_type.72, (f32[1,5,2,256]{3,1,2,0:T(8,128)S(1)}, f32[1,5,2,256]{3,1,2,0:T(8,128)S(1)}, f32[1,5,2,256,128]{4,3,2,1,0:T(8,128)S(1)}) %tuple.77, (s32[]{:T(128)}, ...), branch_computations={%region_11.11_spmd, %region_12.14_spmd} | conditional | flops 682238976 | bytes 19451948 | solution.py:124
  272.4 6.0 %conditional.5 = ((f32[1,5,2,256]{3,1,2,0:T(8,128)S(1)}, f32[1,5,2,256]{3,1,2,0:T(8,128)S(1)}, f32[1,5,2,256,128]{4,3,2,1,0:T(8,128)S(1)})) conditional(s32[]{:T(128)} %convert_element_type.72, (f32[1,5,2,256]{3,1,2,0:T(8,128)S(1)}, f32[1,5,2,256]{3,1,2,0:T(8,128)S(1)}, f32[1,5,2,256,128]{4,3,2,1,0:T(8,128)S(1)}) %tuple.77, (s32[]{:T(128)}, ...), branch_computations={%region_11.11_spmd, %region_12.14_spmd} | conditional | flops 682238976 | bytes 19451948 | solution.py:124
  280.2 6.0 %conditional.5 = ((f32[1,5,2,256]{3,1,2,0:T(8,128)S(1)}, f32[1,5,2,256]{3,1,2,0:T(8,128)S(1)}, f32[1,5,2,256,128]{4,3,2,1,0:T(8,128)S(1)})) conditional(s32[]{:T(128)} %convert_element_type.72, (f32[1,5,2,256]{3,1,2,0:T(8,128)S(1)}, f32[1,5,2,256]{3,1,2,0:T(8,128)S(1)}, f32[1,5,2,256,128]{4,3,2,1,0:T(8,128)S(1)}) %tuple.77, (s32[]{:T(128)}, ...), branch_computations={%region_11.11_spmd, %region_12.14_spmd} | conditional | flops 682238976 | bytes 19451948 | solution.py:124
  288.1 6.0 %conditional.5 = ((f32[1,5,2,256]{3,1,2,0:T(8,128)S(1)}, f32[1,5,2,256]{3,1,2,0:T(8,128)S(1)}, f32[1,5,2,256,128]{4,3,2,1,0:T(8,128)S(1)})) conditional(s32[]{:T(128)} %convert_element_type.72, (f32[1,5,2,256]{3,1,2,0:T(8,128)S(1)}, f32[1,5,2,256]{3,1,2,0:T(8,128)S(1)}, f32[1,5,2,256,128]{4,3,2,1,0:T(8,128)S(1)}) %tuple.77, (s32[]{:T(128)}, ...), branch_computations={%region_11.11_spmd, %region_12.14_spmd} | conditional | flops 682238976 | bytes 19451948 | solution.py:124
  296.0 6.0 %conditional.5 = ((f32[1,5,2,256]{3,1,2,0:T(8,128)S(1)}, f32[1,5,2,256]{3,1,2,0:T(8,128)S(1)}, f32[1,5,2,256,128]{4,3,2,1,0:T(8,128)S(1)})) conditional(s32[]{:T(128)} %convert_element_type.72, (f32[1,5,2,256]{3,1,2,0:T(8,128)S(1)}, f32[1,5,2,256]{3,1,2,0:T(8,128)S(1)}, f32[1,5,2,256,128]{4,3,2,1,0:T(8,128)S(1)}) %tuple.77, (s32[]{:T(128)}, ...), branch_computations={%region_11.11_spmd, %region_12.14_spmd} | conditional | flops 682238976 | bytes 19451948 | solution.py:124
  303.9 6.0 %conditional.5 = ((f32[1,5,2,256]{3,1,2,0:T(8,128)S(1)}, f32[1,5,2,256]{3,1,2,0:T(8,128)S(1)}, f32[1,5,2,256,128]{4,3,2,1,0:T(8,128)S(1)})) conditional(s32[]{:T(128)} %convert_element_type.72, (f32[1,5,2,256]{3,1,2,0:T(8,128)S(1)}, f32[1,5,2,256]{3,1,2,0:T(8,128)S(1)}, f32[1,5,2,256,128]{4,3,2,1,0:T(8,128)S(1)}) %tuple.77, (s32[]{:T(128)}, ...), branch_computations={%region_11.11_spmd, %region_12.14_spmd} | conditional | flops 682238976 | bytes 19451948 | solution.py:124
  311.8 6.0 %conditional.5 = ((f32[1,5,2,256]{3,1,2,0:T(8,128)S(1)}, f32[1,5,2,256]{3,1,2,0:T(8,128)S(1)}, f32[1,5,2,256,128]{4,3,2,1,0:T(8,128)S(1)})) conditional(s32[]{:T(128)} %convert_element_type.72, (f32[1,5,2,256]{3,1,2,0:T(8,128)S(1)}, f32[1,5,2,256]{3,1,2,0:T(8,128)S(1)}, f32[1,5,2,256,128]{4,3,2,1,0:T(8,128)S(1)}) %tuple.77, (s32[]{:T(128)}, ...), branch_computations={%region_11.11_spmd, %region_12.14_spmd} | conditional | flops 682238976 | bytes 19451948 | solution.py:124
  319.7 6.0 %conditional.5 = ((f32[1,5,2,256]{3,1,2,0:T(8,128)S(1)}, f32[1,5,2,256]{3,1,2,0:T(8,128)S(1)}, f32[1,5,2,256,128]{4,3,2,1,0:T(8,128)S(1)})) conditional(s32[]{:T(128)} %convert_element_type.72, (f32[1,5,2,256]{3,1,2,0:T(8,128)S(1)}, f32[1,5,2,256]{3,1,2,0:T(8,128)S(1)}, f32[1,5,2,256,128]{4,3,2,1,0:T(8,128)S(1)}) %tuple.77, (s32[]{:T(128)}, ...), branch_computations={%region_11.11_spmd, %region_12.14_spmd} | conditional | flops 682238976 | bytes 19451948 | solution.py:124
  327.6 6.0 %conditional.5 = ((f32[1,5,2,256]{3,1,2,0:T(8,128)S(1)}, f32[1,5,2,256]{3,1,2,0:T(8,128)S(1)}, f32[1,5,2,256,128]{4,3,2,1,0:T(8,128)S(1)})) conditional(s32[]{:T(128)} %convert_element_type.72, (f32[1,5,2,256]{3,1,2,0:T(8,128)S(1)}, f32[1,5,2,256]{3,1,2,0:T(8,128)S(1)}, f32[1,5,2,256,128]{4,3,2,1,0:T(8,128)S(1)}) %tuple.77, (s32[]{:T(128)}, ...), branch_computations={%region_11.11_spmd, %region_12.14_spmd} | conditional | flops 682238976 | bytes 19451948 | solution.py:124
  335.4 6.0 %conditional.5 = ((f32[1,5,2,256]{3,1,2,0:T(8,128)S(1)}, f32[1,5,2,256]{3,1,2,0:T(8,128)S(1)}, f32[1,5,2,256,128]{4,3,2,1,0:T(8,128)S(1)})) conditional(s32[]{:T(128)} %convert_element_type.72, (f32[1,5,2,256]{3,1,2,0:T(8,128)S(1)}, f32[1,5,2,256]{3,1,2,0:T(8,128)S(1)}, f32[1,5,2,256,128]{4,3,2,1,0:T(8,128)S(1)}) %tuple.77, (s32[]{:T(128)}, ...), branch_computations={%region_11.11_spmd, %region_12.14_spmd} | conditional | flops 682238976 | bytes 19451948 | solution.py:124
  343.1 11.5 %convolution_convert_fusion = bf16[768,5120]{1,0:T(8,128)(2,1)} fusion(bf16[640,5120]{1,0:T(8,128)(2,1)} %param.23, bf16[512,640]{0,1:T(8,128)(2,1)S(1)} %bitcast.181, bf16[256,640]{0,1:T(8,128)(2,1)S(1)} %bitcast.183), kind=kOutput, calls=%fused_computation.56 | convolution fusion | flops 5039063040 | bytes 15400960 | tf_op jit(solution)/shard_map/dot_general | solution.py:152
  354.6 10.6 %copy.54 = bf16[768,5120]{0,1:T(8,128)(2,1)} copy(bf16[768,5120]{1,0:T(8,128)(2,1)} %convolution_convert_fusion) | data formatting | bytes 15728640
  365.2 89.0 %reduce-scatter.4.cloned.1.call-done = bf16[640,768]{1,0:T(8,128)(2,1)} async-done(((bf16[5120,768]{1,0:T(8,128)(2,1)}), bf16[640,768]{1,0:T(8,128)(2,1)}) %reduce-scatter.4.cloned.1.call-update) | async-done | bytes 983056
  (418 shorter events, 225.7 us)
Async XLA Ops:
  7.2 5.3 %copy-start = (bf16[2,256,128]{2,1,0:T(8,128)(2,1)S(1)}, bf16[2,256,128]{2,1,0:T(8,128)(2,1)}, u32[]{:S(2)}) copy-start(bf16[2,256,128]{2,1,0:T(8,128)(2,1)} %param.20) | copy-start | bytes 393220
  7.2 56.0 %all-gather.3.cloned.1.call-start = ((), (), s32[]{:S(2)}) async-start(), calls=%async_computation.1 | async-start | bytes 2162688 | tf_op jit(solution)/shard_map/all_gather | solution.py:129
  7.9 109.6 %all-gather.5.cloned.1.call-start = ((), (), s32[]{:S(2)}) async-start(), calls=%async_computation.2 | async-start | bytes 2162688 | tf_op jit(solution)/shard_map/all_gather | solution.py:130
  8.7 445.5 %reduce-scatter.4.cloned.1.call-start = ((), (), s32[]{:S(2)}) async-start(), calls=%async_computation.3 | async-start | bytes 8847360
  12.0 0.9 copy-start.3
  13.0 1.5 copy-start.2
  13.0 1.5 copy-start.1
Sparse Core Ops, SparseCore 0:
  10.6 52.5 all-gather.2
  65.7 51.7 all-gather.4
  365.3 88.8 reduce-scatter.3
where the time goes:
time: 471 us; the launch traced here: 465 us
  waiting for transfers between devices  190 us (40%)
  matrix products  137 us (29%)
  loops' own time  43.9 us (9%)
  local copies, waits for them, and re-layouts  40.5 us (9%)
  other arithmetic  39.2 us (8%)
  between operations  13.9 us (3%)
    unnamed x4, waiting for transfers between devices  90.4 us
    dot_general x32, matrix products, absorb(): jnp.einsum(spec, weights.astype(jnp.bfloat16), value_list, preferred_elem...  72 us
    all_gather x1, waiting for transfers between devices, per_device(): lax.all_gather(solution_values, 'seq', axis=0, tiled=True)  54.3 us
    all_gather x1, waiting for transfers between devices, per_device(): lax.all_gather(solution_keys, 'seq', axis=0, tiled=True)  45.1 us
    another operation x2, loops' own time, over_blocks(): lax.scan(advance, carry, (key_blocks, value_blocks, jnp.arange(block_coun...  41.4 us
    dot_general x16, matrix products, critique_attend(): jnp.einsum('clngd,knd->ngclk', crit_queries, key_list, preferred_element_...  28.9 us
    dot_general x16, matrix products, solution_attend(): jnp.einsum('rngd,knd->ngrk', sol_queries, key_list, preferred_element_typ...  23.6 us
    another operation x16, other arithmetic  21.6 us
  transfers between devices with their start and end apart: 3, of which 3 were waited for; matrix products, arithmetic and copies ran while one was open for 2% of the time, Pallas kernels for 0%

commit v1 on v0

v1 whole, which is shorter than its diff:
```python
import functools
import math

import jax
import jax.numpy as jnp
from jax import lax
from jax.experimental import pallas as pl
from jax.experimental.pallas import tpu as pltpu
from jax.sharding import PartitionSpec as P

HEAD = 128
HEADS = 5
ROWS = 256
WIDE = HEADS * ROWS
COLS = HEADS * HEAD
KEYS = 512
NEG = -1e30
SCALE = math.log2(math.e) / math.sqrt(HEAD)
FUSED = True

ORDER = (
    (0, -1), (0, 1), (-1, 0), (1, 0), (0, 2), (2, 0), (-1, -1), (-1, 1),
    (1, -1), (1, 1), (-1, 2), (1, 2), (2, -1), (2, 1), (2, 2),
)
STEPS = (
    (("z", "m"), ("z", "p"), ("y", "0", "m"), ("y", "0", "p")),
    (("z", "2"),),
    (("y", "0", "2"),),
    (("y", "m", "m"),),
    (("y", "m", "p"),),
    (("y", "p", "m"), ("y", "p", "p")),
    (("y", "m", "2"),),
    (("y", "p", "2"),),
    (("y", "2", "m"),),
    (("y", "2", "p"),),
    (("y", "2", "2"),),
    (), (), (), (),
)


def pick(index, table):
    value = jnp.int32(table[0])
    for at, entry in enumerate(table[1:], 1):
        value = jnp.where(index == at, jnp.int32(entry), value)
    return value


def kernel(
    sol_q, sol_k, sol_v, crit_q, crit_k, crit_v, bnd, w_hbm, out,
    kv, own_kv, sbuf, acc, top, att, w2, relay, psend, precv, pown,
    kv_send, kv_recv, w_send, w_recv, wl_sem, x_send, x_recv, p_send, p_recv,
):
    s = lax.axis_index("seq")
    t = lax.axis_index("tp")
    a, b, c = s // 8, (s // 2) % 4, s % 2
    ch = s // 2
    sib = s + 1 - 2 * c
    zl, x = t // 4, t % 4
    d = 1 - 2 * c

    def seq_at(za, yb):
        return za * 8 + yb * 2 + c

    def hop(v, by):
        return (v + by + 8) % 4

    def rel(v, which):
        return {"0": v, "m": hop(v, -d), "p": hop(v, d), "2": hop(v, 2)}[which]

    def tp_at(xx):
        return zl * 4 + xx

    partner = (1 - zl) * 4 + x

    def remote(src, dst, ssem, rsem, seq=None, tp=None):
        return pltpu.make_async_remote_copy(
            src_ref=src, dst_ref=dst, send_sem=ssem, recv_sem=rsem,
            device_id={"seq": s if seq is None else seq, "tp": t if tp is None else tp},
            device_id_type=pl.DeviceIdType.MESH,
        )

    kv[s, 0:256, :] = sol_k[...]
    kv[s, 256:384, :] = sol_v[0:128, :].T
    kv[s, 384:512, :] = sol_v[128:256, :].T
    for i in range(2):
        own_kv[i, 0:256, :] = crit_k[i]
        own_kv[i, 256:384, :] = crit_v[i, 0:128, :].T
        own_kv[i, 384:512, :] = crit_v[i, 128:256, :].T

    barrier = pltpu.get_barrier_semaphore()
    friends = [
        (seq_at(hop(a, 1), b), t), (seq_at(hop(a, -1), b), t),
        (seq_at(a, hop(b, 1)), t), (seq_at(a, hop(b, -1)), t), (sib, t),
    ]
    if FUSED:
        friends += [(s, tp_at(hop(x, 1))), (s, tp_at(hop(x, -1))), (s, partner)]
    for fs, ft in friends:
        pl.semaphore_signal(
            barrier, inc=1, device_id={"seq": fs, "tp": ft}, device_id_type=pl.DeviceIdType.MESH
        )
    pl.semaphore_wait(barrier, len(friends))

    sent = [0]

    def send_kv(block, to):
        k = sent[0]
        sent[0] += 1
        remote(kv.at[block], kv.at[block], kv_send.at[k], kv_recv.at[block], seq=to).start()

    def wait_kv(block):
        remote(kv.at[block], kv.at[block], kv_send.at[0], kv_recv.at[block], seq=sib).wait_recv()

    def send_y(block):
        send_kv(block, seq_at(a, hop(b, d)))
        send_kv(block, seq_at(a, hop(b, -d)))

    send_kv(s, seq_at(hop(a, d), b))
    send_kv(s, seq_at(hop(a, -d), b))
    send_y(s)
    send_kv(s, sib)

    def service(item):
        if item[0] == "z":
            block = seq_at(rel(a, item[1]), b)
            wait_kv(block)
            if item[1] == "m":
                send_kv(block, seq_at(hop(a, d), b))
            send_y(block)
            send_kv(block, sib)
        else:
            block = seq_at(rel(a, item[1]), rel(b, item[2]))
            wait_kv(block)
            if item[2] == "m":
                send_kv(block, seq_at(a, hop(b, d)))
            send_kv(block, sib)

    def w_from(rows, count, group):
        return w_hbm.at[pl.ds(rows, count), pl.ds(pl.multiple_of(group * COLS, 128), COLS)]

    half = pl.multiple_of(c * 320, 16)

    def w_part(owner, which_half):
        return w2.at[owner, :, pl.ds(pl.multiple_of(which_half * 320, 16), 320), :]

    if FUSED:
        for i in range(2):
            remote(
                w_from(half, 320, i * 4 + hop(x, 2)), relay.at[i],
                w_send.at[i], w_recv.at[i], tp=tp_at(hop(x, d)),
            ).start()
        for n, by in enumerate((d, -d)):
            for i in range(2):
                remote(
                    w_from(half, 320, i * 4 + hop(x, by)),
                    w2.at[x, i, pl.ds(half, 320), :],
                    w_send.at[2 + n * 2 + i], w_recv.at[2 + n * 2 + i], tp=tp_at(hop(x, by)),
                ).start()
        for i in range(2):
            pltpu.make_async_copy(w_from(0, COLS, i * 4 + x), w2.at[x, i], wl_sem.at[i]).start()

    def w_forward():
        for i in range(2):
            remote(
                relay.at[i], relay.at[i], w_send.at[0], w_recv.at[i], tp=tp_at(hop(x, d))
            ).wait_recv()
        remote(
            relay, w_part(hop(x, -d), c), w_send.at[6], w_recv.at[6], tp=tp_at(hop(x, d))
        ).start()

    def w_share_near():
        for n, by in enumerate((-d, d)):
            owner = hop(x, by)
            for i in range(2):
                ref = w2.at[owner, i, pl.ds(half, 320), :]
                remote(
                    ref, ref, w_send.at[0], w_recv.at[2 + n * 2 + i], tp=tp_at(owner)
                ).wait_recv()
            remote(
                w_part(owner, c), w_part(owner, c), w_send.at[7 + n], w_recv.at[7 + n], seq=sib
            ).start()

    def w_share_far():
        owner = hop(x, 2)
        ref = w_part(owner, c)
        remote(ref, ref, w_send.at[0], w_recv.at[6], tp=tp_at(hop(x, d))).wait_recv()
        remote(ref, ref, w_send.at[9], w_recv.at[9], seq=sib).start()

    def w_ready():
        for n, by in enumerate((d, -d)):
            ref = w_part(hop(x, by), 1 - c)
            remote(ref, ref, w_send.at[0], w_recv.at[7 + n], seq=sib).wait_recv()
        ref = w_part(hop(x, 2), 1 - c)
        remote(ref, ref, w_send.at[0], w_recv.at[9], seq=sib).wait_recv()
        for i in range(2):
            pltpu.make_async_copy(w_from(0, COLS, i * 4 + x), w2.at[x, i], wl_sem.at[i]).wait()

    def query(g, h):
        if isinstance(g, int) and g == 0:
            return sol_q[:, h * HEAD:(h + 1) * HEAD]
        return crit_q[g - 1, :, h * HEAD:(h + 1) * HEAD]

    def dot_keys(keys, g, h):
        return lax.dot_general(
            keys, query(g, h), (((1,), (1,)), ((), ())), preferred_element_type=jnp.float32
        )

    def keys_of(j):
        return kv[pl.ds(2 * j, 2), 0:256, :].reshape(KEYS, HEAD)

    def values_of(j):
        parts = [kv[2 * j, 256:384, :], kv[2 * j, 384:512, :],
                 kv[2 * j + 1, 256:384, :], kv[2 * j + 1, 384:512, :]]
        return jnp.concatenate(
            [jnp.concatenate(parts, axis=1), jnp.ones((16, KEYS), jnp.bfloat16)], axis=0
        )

    def absorb(h, scores, values):
        cs = slice(h * ROWS, (h + 1) * ROWS)
        old = top[0:1, cs]
        new = jnp.maximum(old, jnp.max(scores, axis=0, keepdims=True))
        rescale = jnp.exp2((old - new) * SCALE)
        weights = jnp.exp2((scores - new) * SCALE).astype(jnp.bfloat16)
        acc[:, cs] = acc[:, cs] * rescale + lax.dot_general(
            values, weights, (((1,), (0,)), ((), ())), preferred_element_type=jnp.float32
        )
        top[0:1, cs] = new

    def begin(g):
        top[...] = jnp.full_like(top, NEG)
        acc[...] = jnp.zeros_like(acc)
        keys = keys_of(ch)
        key_at = lax.broadcasted_iota(jnp.int32, (KEYS, ROWS), 0)
        if isinstance(g, int) and g == 0:
            allowed = key_at <= lax.broadcasted_iota(jnp.int32, (KEYS, ROWS), 1) + 256 * c
        else:
            allowed = key_at < bnd[2 * s + g - 1] - KEYS * ch
        for h in range(HEADS):
            sbuf[h] = jnp.where(allowed, dot_keys(keys, g, h), NEG)

    def advance(g, now, then):
        values, keys = values_of(now), keys_of(then)
        for h in range(HEADS):
            absorb(h, sbuf[h], values)
            sbuf[h] = dot_keys(keys, g, h)

    def only_keys(g, then):
        keys = keys_of(then)
        for h in range(HEADS):
            sbuf[h] = dot_keys(keys, g, h)

    def last(now):
        values = values_of(now)
        for h in range(HEADS):
            absorb(h, sbuf[h], values)

    def finish(g):
        for h in range(HEADS):
            cs = slice(h * ROWS, (h + 1) * ROWS)
            value = acc[0:HEAD, cs] * (1.0 / acc[HEAD:HEAD + 1, cs])
            att[g, x, :, h * HEAD:(h + 1) * HEAD] = value.T.astype(jnp.bfloat16)

    def x_start(g):
        ref = att.at[g, x]
        remote(ref, ref, x_send.at[3 * g], x_recv.at[4 * g + x], tp=tp_at(hop(x, d))).start()
        remote(ref, ref, x_send.at[3 * g + 1], x_recv.at[4 * g + x], tp=tp_at(hop(x, -d))).start()

    def x_wait(g, owner):
        ref = att.at[g, owner]
        remote(ref, ref, x_send.at[0], x_recv.at[4 * g + owner], tp=tp_at(hop(x, d))).wait_recv()

    def x_forward(g):
        owner = hop(x, -d)
        x_wait(g, owner)
        ref = att.at[g, owner]
        remote(
            ref, ref, x_send.at[3 * g + 2], x_recv.at[4 * g + owner], tp=tp_at(hop(x, d))
        ).start()

    def project(g):
        x_wait(g, hop(x, d))
        x_wait(g, hop(x, 2))
        for mine in (False, True):
            z = zl if mine else 1 - zl
            total = jnp.zeros((ROWS, COLS), jnp.float32)
            for o in range(4):
                total += jnp.dot(att[g, o], w2[o, z], preferred_element_type=jnp.float32)
            if mine:
                pown[g] = total
            else:
                psend[g] = total.astype(jnp.bfloat16)
                remote(
                    psend.at[g], precv.at[g], p_send.at[g], p_recv.at[g], tp=partner
                ).start()

    def complete(g):
        remote(psend.at[g], precv.at[g], p_send.at[g], p_recv.at[g], tp=partner).wait_recv()
        out[g] = (pown[g] + precv[g].astype(jnp.float32)).astype(jnp.bfloat16)

    wait_kv(sib)
    begin(0)

    def slot(e, carry):
        before, before_ok = carry
        for at, items in enumerate(STEPS):
            if items:
                @pl.when(e == at)
                def _(items=items):
                    for item in items:
                        service(item)
        j = hop(a, pick(e, [o[0] for o in ORDER])) * 4 + hop(b, pick(e, [o[1] for o in ORDER]))
        wait_kv(2 * j + 1 - c)
        ok = j < ch

        @pl.when(before_ok)
        def _():
            advance(0, before, j)

        @pl.when(jnp.logical_and(jnp.logical_not(before_ok), ok))
        def _():
            only_keys(0, j)

        return j, ok

    before, before_ok = lax.fori_loop(0, 15, slot, (ch, jnp.bool_(True)))

    @pl.when(before_ok)
    def _():
        last(before)

    finish(0)
    if FUSED:
        x_start(0)
        w_forward()

    def group(g, _):
        begin(g)

        def step(i, _):
            if FUSED:
                @pl.when(i == 4)
                def _():
                    x_forward(g - 1)

                @pl.when(jnp.logical_and(i == 5, g == 1))
                def _():
                    w_share_near()

                @pl.when(jnp.logical_and(i == 11, g == 1))
                def _():
                    w_share_far()
            advance(g, jnp.where(i == 0, ch, i - 1), i)
            return 0

        lax.fori_loop(0, ch, step, 0)
        last(jnp.where(ch == 0, ch, ch - 1))
        keys = own_kv[g - 1, 0:256, :]
        values = jnp.concatenate(
            [
                jnp.concatenate([own_kv[g - 1, 256:384, :], own_kv[g - 1, 384:512, :]], axis=1),
                jnp.ones((16, 256), jnp.bfloat16),
            ],
            axis=0,
        )
        shape = (256, ROWS)
        allowed = lax.broadcasted_iota(jnp.int32, shape, 0) <= lax.broadcasted_iota(jnp.int32, shape, 1)
        for h in range(HEADS):
            sbuf[h, 0:256, :] = jnp.where(allowed, dot_keys(keys, g, h), NEG)
        for h in range(HEADS):
            absorb(h, sbuf[h, 0:256, :], values)
        finish(g)
        if FUSED:
            x_start(g)

            @pl.when(ch <= 4)
            def _():
                x_forward(g - 1)

            @pl.when(g == 1)
            def _():
                @pl.when(ch <= 5)
                def _():
                    w_share_near()

                @pl.when(ch <= 11)
                def _():
                    w_share_far()

                w_ready()

            project(g - 1)
        return 0

    lax.fori_loop(1, 3, group, 0)
    if FUSED:
        x_forward(2)
        complete(0)
        complete(1)
        project(2)
        complete(2)
    else:
        for g in range(3):
            out[g] = att[g, x]

    for k in range(sent[0]):
        remote(kv.at[0], kv.at[0], kv_send.at[k], kv_recv.at[0], seq=sib).wait_send()
    if FUSED:
        for i in range(6):
            remote(relay.at[0], relay.at[0], w_send.at[i], w_recv.at[0], tp=partner).wait_send()
        for i in range(6, 10):
            remote(relay, relay, w_send.at[i], w_recv.at[0], tp=partner).wait_send()
        for i in range(9):
            ref = att.at[0, 0]
            remote(ref, ref, x_send.at[i], x_recv.at[0], tp=partner).wait_send()
        for g in range(3):
            remote(psend.at[g], precv.at[g], p_send.at[g], p_recv.at[g], tp=partner).wait_send()


def per_device(
    sol_q, solution_keys, solution_values, crit_q, crit_k, critique_values, boundary, w_out
):
    vmem = pl.BlockSpec(memory_space=pltpu.VMEM)
    bf, f32 = jnp.bfloat16, jnp.float32
    dma = pltpu.SemaphoreType.DMA
    result = pl.pallas_call(
        kernel,
        out_shape=jax.ShapeDtypeStruct((3, ROWS, COLS), bf),
        in_specs=[vmem] * 6 + [pl.BlockSpec(memory_space=pltpu.SMEM), pl.BlockSpec(memory_space=pl.ANY)],
        out_specs=vmem,
        scratch_shapes=[
            pltpu.VMEM((32, 512, HEAD), bf),
            pltpu.VMEM((2, 512, HEAD), bf),
            pltpu.VMEM((HEADS, KEYS, ROWS), f32),
            pltpu.VMEM((HEAD + 16, WIDE), f32),
            pltpu.VMEM((8, WIDE), f32),
            pltpu.VMEM((3, 4, ROWS, COLS), bf),
            pltpu.VMEM((4, 2, COLS, COLS), bf),
            pltpu.VMEM((2, 320, COLS), bf),
            pltpu.VMEM((3, ROWS, COLS), bf),
            pltpu.VMEM((3, ROWS, COLS), bf),
            pltpu.VMEM((3, ROWS, COLS), f32),
            dma((31,)), dma((32,)), dma((10,)), dma((10,)), dma((2,)),
            dma((9,)), dma((12,)), dma((3,)), dma((3,)),
        ],
        compiler_params=pltpu.CompilerParams(
            collective_id=0, has_side_effects=True, vmem_limit_bytes=50 * 2**20
        ),
        cost_estimate=pl.CostEstimate(
            flops=20_000_000_000, bytes_accessed=16_000_000, transcendentals=32_000_000
        ),
    )(sol_q, solution_keys, solution_values, crit_q, crit_k, critique_values, boundary, w_out)
    if not FUSED:
        partial = jnp.dot(result.reshape(768, COLS), w_out, preferred_element_type=f32)
        result = lax.psum_scatter(
            partial.astype(bf), "tp", scatter_dimension=1, tiled=True
        ).reshape(3, ROWS, COLS)
    return result[0], result[1:]


def solution(mesh):
    in_specs = (
        P("seq", "tp"), P("seq", "tp"), P("seq", "tp"),
        P("seq", None, "tp"), P("seq", None, "tp"), P("seq", None, "tp"),
        P(), P("tp", None),
    )
    out_specs = (P("seq", "tp"), P("seq", None, "tp"))
    return jax.shard_map(
        per_device, mesh=mesh, in_specs=in_specs, out_specs=out_specs, check_vma=False
    )
```

time: 471 us -> 116 us (0.25)
  the two profiles are of different devices: /device:TPU:216 before, /device:TPU:66 now
where the time goes in v1:
time: 116 us; the launch traced here: 115 us
  Pallas kernels  107 us (92%)
  local copies, waits for them, and re-layouts  7.84 us (7%)
    pallas_call x1, Pallas kernels, per_device(): pl.pallas_call(kernel, out_shape=jax.ShapeDtypeStruct((3, ROWS, COLS), bf...  107 us
    unnamed x14, local copies, waits for them, and re-layouts  6.19 us

profile of v1, /device:TPU:66, one launch (start us, length us, event | category | flops | bytes accessed | tf_op | source)
XLA Modules:
  0.0 115.3 jit_solution(8869044797456042407)
XLA Ops:
  0.6 0.0 copy-start
  0.6 1.1 copy-done
  1.7 0.0 copy-start.1
  1.7 1.0 copy-done.1
  2.7 0.0 copy-start.2
  2.7 0.9 copy-done.2
  3.6 0.0 copy-start.3
  3.6 0.9 copy-done.3
  4.5 0.0 copy-start.4
  4.5 0.8 copy-done.4
  5.3 0.0 copy-start.5
  5.3 0.8 copy-done.5
  6.2 0.0 copy-start.6
  6.2 0.7 copy-done.6
  6.8 106.8 %shard_map.95 = bf16[3,256,640]{2,1,0:T(8,128)(2,1)S(1)} custom-call(bf16[256,640]{1,0:T(8,128)(2,1)S(1)} %copy-done.1, bf16[256,128]{1,0:T(8,128)(2,1)S(1)} %copy-done.4, bf16[256,128]{1,0:T(8,128)(2,1)S(1)} %copy-done.5, bf16[2,256,640]{2,1,0:T(8,128)(2,1)S(1)} %copy-done, bf16[2,256,128]{2,1,0:T(8,128)(2,1)S(1)} %copy-done.2, ...), custom_call_target="tpu_custom_call" | custom-call | flops 20000000000 | bytes 16000000 | tf_op jit(solution)/shard_map/pallas_call | solution.py:424
  113.6 0.8 slice_bitcast_fusion
  114.4 0.9 slice.7
Async XLA Ops:
  0.6 1.1 copy-start
  1.7 1.0 copy-start.1
  2.7 0.9 copy-start.2
  3.6 0.9 copy-start.3
  4.5 0.8 copy-start.4
  5.3 0.8 copy-start.5
  6.2 0.7 copy-start.6

commit v2 on v1

v2 whole, which is shorter than its diff:
```python
import functools
import math

import jax
import jax.numpy as jnp
from jax import lax
from jax.experimental import pallas as pl
from jax.experimental.pallas import tpu as pltpu
from jax.sharding import PartitionSpec as P

HEAD = 128
HEADS = 5
ROWS = 256
WIDE = HEADS * ROWS
COLS = HEADS * HEAD
KEYS = 512
NEG = -1e30
SCALE = math.log2(math.e) / math.sqrt(HEAD)
VMEM_LIMIT = 63 * 2**20
KV = True
ATT = True
WX = True
XX = True
PJ = True

ORDER = (
    (0, -1), (0, 1), (-1, 0), (1, 0), (0, 2), (2, 0), (-1, -1), (-1, 1),
    (1, -1), (1, 1), (-1, 2), (1, 2), (2, -1), (2, 1), (2, 2),
)
STEPS = (
    (("y", "0", "m"), ("z", "m"), ("z", "p"), ("y", "0", "p")),
    (),
    (("y", "0", "2"),),
    (("z", "2"), ("w",)),
    (),
    (("y", "m", "m"), ("y", "p", "m")),
    (("y", "m", "p"), ("y", "p", "p")),
    (),
    (("y", "2", "m"),),
    (("y", "2", "p"),),
    (("y", "m", "2"), ("y", "p", "2")),
    (("y", "2", "2"),),
    (), (), (),
)


def pick(index, table):
    value = jnp.int32(table[0])
    for at, entry in enumerate(table[1:], 1):
        value = jnp.where(index == at, jnp.int32(entry), value)
    return value


def kernel(
    sol_q_in, sol_k_in, sol_v_in, crit_q_in, crit_k_in, crit_v_in, bnd_in, w_hbm, sol_out, crit_out,
    sol_q, sol_k, sol_v, crit_q, crit_k, crit_v, bnd, kv, own_kv, sbuf, acc, top, att, wown, wpar,
    hold, msend, mrecv, done,
    in_sem, out_sem, kv_send, kv_recv, w_send, w_recv, z_send, z_recv, m_send, m_recv,
):
    s = lax.axis_index("seq")
    t = lax.axis_index("tp")
    a, b, c = s // 8, (s // 2) % 4, s % 2
    ch = s // 2
    sib = s + 1 - 2 * c
    zl, x = t // 4, t % 4
    d = 1 - 2 * c

    def seq_at(za, yb):
        return za * 8 + yb * 2 + c

    def hop(v, by):
        return (v + by + 8) % 4

    def rel(v, which):
        return {"0": v, "m": hop(v, -d), "p": hop(v, d), "2": hop(v, 2)}[which]

    def tp_at(xx):
        return zl * 4 + xx

    partner = (1 - zl) * 4 + x
    beyond = seq_at(hop(a, 2 * zl - 1), b)

    def remote(src, dst, ssem, rsem, seq=None, tp=None):
        return pltpu.make_async_remote_copy(
            src_ref=src, dst_ref=dst, send_sem=ssem, recv_sem=rsem,
            device_id={"seq": s if seq is None else seq, "tp": t if tp is None else tp},
            device_id_type=pl.DeviceIdType.MESH,
        )

    loads = [
        pltpu.make_async_copy(src, dst, in_sem.at[k])
        for k, (src, dst) in enumerate((
            (sol_k_in, sol_k), (sol_v_in, sol_v), (sol_q_in, sol_q), (crit_k_in, crit_k),
            (crit_v_in, crit_v), (crit_q_in, crit_q), (bnd_in, bnd),
            (w_hbm.at[:, pl.ds(pl.multiple_of(zl * 2560, 128), 2560)], wown),
        ))
    ]
    for load in loads:
        load.start()

    barrier = pltpu.get_barrier_semaphore()
    friends = [
        (seq_at(hop(a, 1), b), t), (seq_at(hop(a, -1), b), t),
        (seq_at(a, hop(b, 1)), t), (seq_at(a, hop(b, -1)), t), (sib, t),
    ]
    friends += [(s, tp_at(hop(x, 1))), (s, tp_at(hop(x, -1))), (s, partner), (beyond, partner)]
    for fs, ft in friends:
        pl.semaphore_signal(
            barrier, inc=1, device_id={"seq": fs, "tp": ft}, device_id_type=pl.DeviceIdType.MESH
        )
    loads[0].wait()
    loads[1].wait()
    kv[s, 0:256, :] = sol_k[...]
    kv[s, 256:384, :] = sol_v[0:128, :].T
    kv[s, 384:512, :] = sol_v[128:256, :].T
    pl.semaphore_wait(barrier, len(friends))

    sent = [0]

    def send_kv(block, to):
        if not KV:
            return
        k = sent[0]
        sent[0] += 1
        remote(kv.at[block], kv.at[block], kv_send.at[k], kv_recv.at[block], seq=to).start()

    def wait_kv(block):
        if not KV:
            return
        remote(kv.at[block], kv.at[block], kv_send.at[0], kv_recv.at[block], seq=sib).wait_recv()

    def send_y(block):
        send_kv(block, seq_at(a, hop(b, d)))
        send_kv(block, seq_at(a, hop(b, -d)))

    send_kv(s, seq_at(hop(a, d), b))
    send_kv(s, seq_at(hop(a, -d), b))
    send_y(s)
    send_kv(s, sib)

    def service(item):
        if item[0] == "w":
            w_start()
            return
        if item[0] == "z":
            block = seq_at(rel(a, item[1]), b)
            wait_kv(block)
            if item[1] == "m":
                send_kv(block, seq_at(hop(a, d), b))
            send_y(block)
            send_kv(block, sib)
        else:
            block = seq_at(rel(a, item[1]), rel(b, item[2]))
            wait_kv(block)
            if item[2] == "m":
                send_kv(block, seq_at(a, hop(b, d)))
            send_kv(block, sib)

    def w_copy(n):
        rows = pl.ds(pl.multiple_of(c * 320 + n * 160, 16), 160)
        return remote(
            w_hbm.at[rows, pl.ds(pl.multiple_of((1 - zl) * 2560, 128), 2560)],
            wpar.at[rows, :], w_send.at[n], w_recv.at[n],
            seq=(s, beyond)[n], tp=partner,
        )

    def w_start():
        if WX:
            w_copy(0).start()
            w_copy(1).start()

    def w_shared(which):
        rows = pl.ds(pl.multiple_of(which * 320, 16), 320)
        return remote(wpar.at[rows, :], wpar.at[rows, :], w_send.at[2], w_recv.at[2], seq=sib)

    def w_share():
        if WX:
            w_copy(0).wait_recv()
            w_copy(1).wait_recv()
            w_shared(c).start()

    def w_ready():
        if WX:
            w_shared(1 - c).wait_recv()
        loads[7].wait()

    def query(g, h):
        if isinstance(g, int) and g == 0:
            return sol_q[:, h * HEAD:(h + 1) * HEAD]
        return crit_q[g - 1, :, h * HEAD:(h + 1) * HEAD]

    def dot_keys(keys, g, h):
        return lax.dot_general(
            keys, query(g, h), (((1,), (1,)), ((), ())), preferred_element_type=jnp.float32
        )

    def keys_of(j):
        return kv[pl.ds(2 * j, 2), 0:256, :].reshape(KEYS, HEAD)

    def values_of(j):
        parts = [kv[2 * j, 256:384, :], kv[2 * j, 384:512, :],
                 kv[2 * j + 1, 256:384, :], kv[2 * j + 1, 384:512, :]]
        return jnp.concatenate(
            [jnp.concatenate(parts, axis=1), jnp.ones((16, KEYS), jnp.bfloat16)], axis=0
        )

    def absorb(u, h, scores, values):
        cs = slice(h * ROWS, (h + 1) * ROWS)
        old = top[u, 0:1, cs]
        new = jnp.maximum(old, jnp.max(scores, axis=0, keepdims=True))
        rescale = jnp.exp2((old - new) * SCALE)
        weights = jnp.exp2((scores - new) * SCALE).astype(jnp.bfloat16)
        acc[u, :, cs] = acc[u, :, cs] * rescale + lax.dot_general(
            values, weights, (((1,), (0,)), ((), ())), preferred_element_type=jnp.float32
        )
        top[u, 0:1, cs] = new

    def begin(u, g):
        if not ATT:
            return
        top[u] = jnp.full((8, WIDE), NEG, jnp.float32)
        acc[u] = jnp.zeros((HEAD + 16, WIDE), jnp.float32)
        keys = keys_of(ch)
        key_at = lax.broadcasted_iota(jnp.int32, (KEYS, ROWS), 0)
        if g == 0:
            allowed = key_at <= lax.broadcasted_iota(jnp.int32, (KEYS, ROWS), 1) + 256 * c
        else:
            allowed = key_at < bnd[2 * s + g - 1] - KEYS * ch
        for h in range(HEADS):
            sbuf[u, h] = jnp.where(allowed, dot_keys(keys, g, h), NEG)

    def advance(units, now, then):
        if not ATT:
            return
        values, keys = values_of(now), keys_of(then)
        for h in range(HEADS):
            for u, g in units:
                absorb(u, h, sbuf[u, h], values)
                sbuf[u, h] = dot_keys(keys, g, h)

    def only_keys(units, then):
        if not ATT:
            return
        keys = keys_of(then)
        for h in range(HEADS):
            for u, g in units:
                sbuf[u, h] = dot_keys(keys, g, h)

    def last(units, now):
        if not ATT:
            return
        values = values_of(now)
        for h in range(HEADS):
            for u, g in units:
                absorb(u, h, sbuf[u, h], values)

    def own(u, g):
        if not ATT:
            return
        keys = own_kv[g - 1, 0:256, :]
        values = jnp.concatenate(
            [
                jnp.concatenate([own_kv[g - 1, 256:384, :], own_kv[g - 1, 384:512, :]], axis=1),
                jnp.ones((16, 256), jnp.bfloat16),
            ],
            axis=0,
        )
        shape = (256, ROWS)
        allowed = lax.broadcasted_iota(jnp.int32, shape, 0) <= lax.broadcasted_iota(jnp.int32, shape, 1)
        for h in range(HEADS):
            sbuf[u, h, 0:256, :] = jnp.where(allowed, dot_keys(keys, g, h), NEG)
        for h in range(HEADS):
            absorb(u, h, sbuf[u, h, 0:256, :], values)

    def finish(u, g):
        if not ATT:
            return
        for h in range(HEADS):
            cs = slice(h * ROWS, (h + 1) * ROWS)
            value = acc[u, 0:HEAD, cs] * (1.0 / acc[u, HEAD:HEAD + 1, cs])
            att[g, 0, :, h * HEAD:(h + 1) * HEAD] = value.astype(jnp.bfloat16).T

    def z_copy(chunk):
        k, g, r, n = chunk
        return remote(
            att.at[g, 0, pl.ds(r, n), :], att.at[g, 1, pl.ds(r, n), :],
            z_send.at[k], z_recv.at[k], tp=partner,
        )

    def m_copy(chunk, kind, to):
        k, g, r, n = chunk
        return remote(
            msend.at[g, kind, pl.ds(r, n), :], mrecv.at[g, kind, pl.ds(r, n), :],
            m_send.at[3 * k + kind], m_recv.at[3 * k + kind], tp=tp_at(to),
        )

    def z_start(chunk):
        if XX:
            z_copy(chunk).start()

    def project(chunk):
        k, g, r, n = chunk
        if XX:
            z_copy(chunk).wait_recv()

        def part(at):
            cols = pl.ds(pl.multiple_of(at * COLS, 128), COLS)
            if not PJ:
                return jnp.zeros((n, COLS), jnp.float32)
            return jnp.dot(
                att[g, 0, r:r + n, :], wown[:, cols], preferred_element_type=jnp.float32
            ) + jnp.dot(att[g, 1, r:r + n, :], wpar[:, cols], preferred_element_type=jnp.float32)

        for kind, at, to in ((0, hop(x, 2), hop(x, d)), (1, hop(x, -d), hop(x, -d))):
            msend[g, kind, r:r + n, :] = part(at).astype(jnp.bfloat16)
            if XX:
                m_copy(chunk, kind, to).start()
        hold[g, 0, r:r + n, :] = part(hop(x, d))
        hold[g, 1, r:r + n, :] = part(x)

    def relay(chunk):
        k, g, r, n = chunk
        if XX:
            m_copy(chunk, 0, hop(x, d)).wait_recv()
        total = hold[g, 0, r:r + n, :] + mrecv[g, 0, r:r + n, :].astype(jnp.float32)
        msend[g, 2, r:r + n, :] = total.astype(jnp.bfloat16)
        if XX:
            m_copy(chunk, 2, hop(x, d)).start()

    def store(chunk):
        k, g, r, n = chunk
        rows = pl.ds(r, n)
        ref = sol_out.at[rows, :] if g == 0 else crit_out.at[g - 1, rows, :]
        return pltpu.make_async_copy(done.at[g, rows, :], ref, out_sem.at[k])

    def complete(chunk):
        k, g, r, n = chunk
        total = hold[g, 1, r:r + n, :]
        for kind in (1, 2):
            if XX:
                m_copy(chunk, kind, hop(x, d)).wait_recv()
            total += mrecv[g, kind, r:r + n, :].astype(jnp.float32)
        done[g, r:r + n, :] = total.astype(jnp.bfloat16)
        store(chunk).start()

    chunks = ((0, 0, 0, 256), (1, 1, 0, 256), (2, 2, 0, 128), (3, 2, 128, 128))

    wait_kv(sib)
    for k in (2, 3, 4, 5, 6):
        loads[k].wait()
    for i in range(2):
        own_kv[i, 0:256, :] = crit_k[i]
        own_kv[i, 256:384, :] = crit_v[i, 0:128, :].T
        own_kv[i, 384:512, :] = crit_v[i, 128:256, :].T
    first = ((0, 0), (1, 1))
    begin(0, 0)
    begin(1, 1)

    def slot(e, carry):
        before, before_ok = carry
        for at, items in enumerate(STEPS):
            if items:
                @pl.when(e == at)
                def _(items=items):
                    for item in items:
                        service(item)
        j = hop(a, pick(e, [o[0] for o in ORDER])) * 4 + hop(b, pick(e, [o[1] for o in ORDER]))
        wait_kv(2 * j + 1 - c)
        ok = j < ch

        @pl.when(before_ok)
        def _():
            advance(first, before, j)

        @pl.when(jnp.logical_and(jnp.logical_not(before_ok), ok))
        def _():
            only_keys(first, j)

        return j, ok

    before, before_ok = lax.fori_loop(0, 15, slot, (ch, jnp.bool_(True)))

    @pl.when(before_ok)
    def _():
        last(first, before)

    finish(0, 0)
    z_start(chunks[0])
    own(1, 1)
    finish(1, 1)

    begin(0, 2)
    second = ((0, 2),)

    def step(i, _):
        for at, work in (
            (1, w_share),
            (2, lambda: z_start(chunks[1])),
            (5, lambda: (w_ready(), project(chunks[0]))),
            (9, lambda: (project(chunks[1]), relay(chunks[0]))),
            (14, lambda: relay(chunks[1])),
        ):
            @pl.when(i == at)
            def _(work=work):
                work()

        @pl.when(i < ch)
        def _():
            advance(second, jnp.where(i == 0, ch, i - 1), i)

        return 0

    lax.fori_loop(0, 15, step, 0)
    last(second, jnp.where(ch == 0, ch, ch - 1))
    own(0, 2)
    finish(0, 2)
    z_start(chunks[2])
    z_start(chunks[3])
    complete(chunks[0])
    project(chunks[2])
    project(chunks[3])
    relay(chunks[2])
    complete(chunks[1])
    relay(chunks[3])
    complete(chunks[2])
    complete(chunks[3])

    for k in range(sent[0]):
        remote(kv.at[0], kv.at[0], kv_send.at[k], kv_recv.at[0], seq=sib).wait_send()
    if WX:
        w_copy(0).wait_send()
        w_copy(1).wait_send()
        w_shared(c).wait_send()
    for chunk in chunks:
        if XX:
            z_copy(chunk).wait_send()
            for kind in range(3):
                m_copy(chunk, kind, hop(x, d)).wait_send()
        store(chunk).wait()


def per_device(
    sol_q, solution_keys, solution_values, crit_q, crit_k, critique_values, boundary, w_out
):
    bf, f32 = jnp.bfloat16, jnp.float32
    dma = pltpu.SemaphoreType.DMA
    hbm = pl.BlockSpec(memory_space=pl.ANY)
    sol_out, crit_out = pl.pallas_call(
        kernel,
        out_shape=(
            jax.ShapeDtypeStruct((ROWS, COLS), bf), jax.ShapeDtypeStruct((2, ROWS, COLS), bf)
        ),
        in_specs=[hbm] * 8,
        out_specs=(hbm, hbm),
        scratch_shapes=[
            pltpu.VMEM((ROWS, COLS), bf),
            pltpu.VMEM((ROWS, HEAD), bf),
            pltpu.VMEM((ROWS, HEAD), bf),
            pltpu.VMEM((2, ROWS, COLS), bf),
            pltpu.VMEM((2, ROWS, HEAD), bf),
            pltpu.VMEM((2, ROWS, HEAD), bf),
            pltpu.SMEM((64,), jnp.int32),
            pltpu.VMEM((32, 512, HEAD), bf),
            pltpu.VMEM((2, 512, HEAD), bf),
            pltpu.VMEM((2, HEADS, KEYS, ROWS), f32),
            pltpu.VMEM((2, HEAD + 16, WIDE), f32),
            pltpu.VMEM((2, 8, WIDE), f32),
            pltpu.VMEM((3, 2, ROWS, COLS), bf),
            pltpu.VMEM((COLS, 4 * COLS), bf),
            pltpu.VMEM((COLS, 4 * COLS), bf),
            pltpu.VMEM((3, 2, ROWS, COLS), f32),
            pltpu.VMEM((3, 3, ROWS, COLS), bf),
            pltpu.VMEM((3, 3, ROWS, COLS), bf),
            pltpu.VMEM((3, ROWS, COLS), bf),
            dma((8,)), dma((4,)), dma((31,)), dma((32,)), dma((3,)), dma((3,)),
            dma((4,)), dma((4,)), dma((12,)), dma((12,)),
        ],
        compiler_params=pltpu.CompilerParams(
            collective_id=0, has_side_effects=True, vmem_limit_bytes=VMEM_LIMIT
        ),
        cost_estimate=pl.CostEstimate(
            flops=20_000_000_000, bytes_accessed=16_000_000, transcendentals=32_000_000
        ),
    )(sol_q, solution_keys, solution_values, crit_q, crit_k, critique_values, boundary, w_out)
    return sol_out, crit_out


def solution(mesh):
    in_specs = (
        P("seq", "tp"), P("seq", "tp"), P("seq", "tp"),
        P("seq", None, "tp"), P("seq", None, "tp"), P("seq", None, "tp"),
        P(), P("tp", None),
    )
    out_specs = (P("seq", "tp"), P("seq", None, "tp"))
    return jax.shard_map(
        per_device, mesh=mesh, in_specs=in_specs, out_specs=out_specs, check_vma=False
    )
```

time: 116 us -> 92.2 us (0.79)
  the two profiles are of different devices: /device:TPU:66 before, /device:TPU:216 now
where the time goes in v2:
time: 92.2 us; the launch traced here: 92.1 us
  Pallas kernels  87.7 us (95%)
  local copies, waits for them, and re-layouts  3.7 us (4%)
    pallas_call x1, Pallas kernels, per_device(): pl.pallas_call(kernel, out_shape=(jax.ShapeDtypeStruct((ROWS, COLS), bf),...  87.7 us
    unnamed x2, local copies, waits for them, and re-layouts  3.7 us

profile of v2, /device:TPU:216, one launch (start us, length us, event | category | flops | bytes accessed | tf_op | source)
XLA Modules:
  0.0 92.1 jit_solution(16532125164188705520)
XLA Ops:
  0.6 87.7 %shard_map.95 = (bf16[256,640]{1,0:T(8,128)(2,1)}, bf16[2,256,640]{2,1,0:T(8,128)(2,1)}) custom-call(bf16[256,640]{1,0:T(8,128)(2,1)} %sol_q_in.1, bf16[256,128]{1,0:T(8,128)(2,1)} %sol_k_in.1, bf16[256,128]{1,0:T(8,128)(2,1)} %sol_v_in.1, bf16[2,256,640]{2,1,0:T(8,128)(2,1)} %crit_q_in.1, bf16[2,256,128]{2,1,0:T(8,128)(2,1)} %crit_k_in.1, ...), custom_call_target="tpu_custom_call" | custom-call | flops 20000000000 | bytes 16000000 | tf_op jit(solution)/shard_map/pallas_call | solution.py:448
  88.4 1.7 %copy.12 = bf16[256,640]{1,0:T(8,128)(2,1)} copy(bf16[256,640]{1,0:T(8,128)(2,1)} %get-tuple-element.4) | data formatting | bytes 655360
  90.1 2.0 %copy.13 = bf16[2,256,640]{2,1,0:T(8,128)(2,1)} copy(bf16[2,256,640]{2,1,0:T(8,128)(2,1)} %get-tuple-element.5) | data formatting | bytes 1310720

commit v3 on v2

--- a/solution.py
+++ b/solution.py
@@ -17,6 +17,7 @@
 NEG = -1e30
 SCALE = math.log2(math.e) / math.sqrt(HEAD)
 VMEM_LIMIT = 63 * 2**20
+AT = (0, 1, 4, 7, 10, 12, 14)
 KV = True
 ATT = True
 WX = True
@@ -28,10 +29,10 @@
     (1, -1), (1, 1), (-1, 2), (1, 2), (2, -1), (2, 1), (2, 2),
 )
 STEPS = (
-    (("y", "0", "m"), ("z", "m"), ("z", "p"), ("y", "0", "p")),
+    (("y", "0", "m"), ("z", "m"), ("z", "p"), ("w",), ("y", "0", "p")),
     (),
     (("y", "0", "2"),),
-    (("z", "2"), ("w",)),
+    (("z", "2"),),
     (),
     (("y", "m", "m"), ("y", "p", "m")),
     (("y", "m", "p"), ("y", "p", "p")),
@@ -215,11 +216,17 @@
         )
         top[u, 0:1, cs] = new
 
-    def begin(u, g):
-        if not ATT:
-            return
+    def reset(unit):
+        if not ATT:
+            return
+        u, g, v = unit
         top[u] = jnp.full((8, WIDE), NEG, jnp.float32)
         acc[u] = jnp.zeros((HEAD + 16, WIDE), jnp.float32)
+
+    def begin(unit):
+        if not ATT:
+            return
+        u, g, v = unit
         keys = keys_of(ch)
         key_at = lax.broadcasted_iota(jnp.int32, (KEYS, ROWS), 0)
         if g == 0:
@@ -227,36 +234,37 @@
         else:
             allowed = key_at < bnd[2 * s + g - 1] - KEYS * ch
         for h in range(HEADS):
-            sbuf[u, h] = jnp.where(allowed, dot_keys(keys, g, h), NEG)
+            sbuf[v, h] = jnp.where(allowed, dot_keys(keys, g, h), NEG)
 
     def advance(units, now, then):
         if not ATT:
             return
         values, keys = values_of(now), keys_of(then)
         for h in range(HEADS):
-            for u, g in units:
-                absorb(u, h, sbuf[u, h], values)
-                sbuf[u, h] = dot_keys(keys, g, h)
+            for u, g, v in units:
+                absorb(u, h, sbuf[v, h], values)
+                sbuf[v, h] = dot_keys(keys, g, h)
 
     def only_keys(units, then):
         if not ATT:
             return
         keys = keys_of(then)
         for h in range(HEADS):
-            for u, g in units:
-                sbuf[u, h] = dot_keys(keys, g, h)
+            for u, g, v in units:
+                sbuf[v, h] = dot_keys(keys, g, h)
 
     def last(units, now):
         if not ATT:
             return
         values = values_of(now)
         for h in range(HEADS):
-            for u, g in units:
-                absorb(u, h, sbuf[u, h], values)
-
-    def own(u, g):
-        if not ATT:
-            return
+            for u, g, v in units:
+                absorb(u, h, sbuf[v, h], values)
+
+    def own(unit):
+        if not ATT:
+            return
+        u, g, v = unit
         keys = own_kv[g - 1, 0:256, :]
         values = jnp.concatenate(
             [
@@ -268,17 +276,20 @@
         shape = (256, ROWS)
         allowed = lax.broadcasted_iota(jnp.int32, shape, 0) <= lax.broadcasted_iota(jnp.int32, shape, 1)
         for h in range(HEADS):
-            sbuf[u, h, 0:256, :] = jnp.where(allowed, dot_keys(keys, g, h), NEG)
-        for h in range(HEADS):
-            absorb(u, h, sbuf[u, h, 0:256, :], values)
-
-    def finish(u, g):
-        if not ATT:
-            return
-        for h in range(HEADS):
-            cs = slice(h * ROWS, (h + 1) * ROWS)
+            sbuf[v, h, 0:256, :] = jnp.where(allowed, dot_keys(keys, g, h), NEG)
+        for h in range(HEADS):
+            absorb(u, h, sbuf[v, h, 0:256, :], values)
+
+    def finish(u, g, half):
+        if not ATT:
+            return
+        for h in range(HEADS):
+            at = h * ROWS + half * HEAD
+            cs = slice(at, at + HEAD)
             value = acc[u, 0:HEAD, cs] * (1.0 / acc[u, HEAD:HEAD + 1, cs])
-            att[g, 0, :, h * HEAD:(h + 1) * HEAD] = value.astype(jnp.bfloat16).T
+            att[g, 0, half * HEAD:(half + 1) * HEAD, h * HEAD:(h + 1) * HEAD] = (
+                value.astype(jnp.bfloat16).T
+            )
 
     def z_copy(chunk):
         k, g, r, n = chunk
@@ -343,18 +354,27 @@
         done[g, r:r + n, :] = total.astype(jnp.bfloat16)
         store(chunk).start()
 
-    chunks = ((0, 0, 0, 256), (1, 1, 0, 256), (2, 2, 0, 128), (3, 2, 128, 128))
-
-    wait_kv(sib)
+    chunks = (
+        (0, 0, 0, 128), (1, 0, 128, 128), (2, 1, 0, 256), (3, 2, 0, 128), (4, 2, 128, 128)
+    )
+
+    first = ((0, 0, 0), (1, 1, 1))
+    second = ((2, 2, 0),)
+    for unit in first + second:
+        reset(unit)
     for k in (2, 3, 4, 5, 6):
         loads[k].wait()
     for i in range(2):
         own_kv[i, 0:256, :] = crit_k[i]
         own_kv[i, 256:384, :] = crit_v[i, 0:128, :].T
         own_kv[i, 384:512, :] = crit_v[i, 128:256, :].T
-    first = ((0, 0), (1, 1))
-    begin(0, 0)
-    begin(1, 1)
+    own(first[1])
+    own(second[0])
+    wait_kv(sib)
+    begin(second[0])
+    last(second, ch)
+    begin(first[0])
+    begin(first[1])
 
     def slot(e, carry):
         before, before_ok = carry
@@ -384,46 +404,56 @@
     def _():
         last(first, before)
 
-    finish(0, 0)
-    z_start(chunks[0])
-    own(1, 1)
-    finish(1, 1)
-
-    begin(0, 2)
-    second = ((0, 2),)
+    for half in range(2):
+        finish(0, 0, half)
+        z_start(chunks[half])
+    finish(1, 1, 0)
+    finish(1, 1, 1)
+
+    @pl.when(ch > 0)
+    def _():
+        only_keys(second, 0)
+
 
     def step(i, _):
         for at, work in (
-            (1, w_share),
-            (2, lambda: z_start(chunks[1])),
-            (5, lambda: (w_ready(), project(chunks[0]))),
-            (9, lambda: (project(chunks[1]), relay(chunks[0]))),
-            (14, lambda: relay(chunks[1])),
+            (AT[0], w_share),
+            (AT[1], lambda: z_start(chunks[2])),
+            (AT[2], lambda: (w_ready(), project(chunks[0]))),
+            (AT[3], lambda: project(chunks[1])),
+            (AT[4], lambda: relay(chunks[0])),
+            (AT[5], lambda: project(chunks[2])),
+            (AT[6], lambda: relay(chunks[1])),
         ):
             @pl.when(i == at)
             def _(work=work):
                 work()
 
-        @pl.when(i < ch)
+        @pl.when(i < ch - 1)
         def _():
-            advance(second, jnp.where(i == 0, ch, i - 1), i)
+            advance(second, i, i + 1)
 
         return 0
 
     lax.fori_loop(0, 15, step, 0)
-    last(second, jnp.where(ch == 0, ch, ch - 1))
-    own(0, 2)
-    finish(0, 2)
-    z_start(chunks[2])
-    z_start(chunks[3])
+
+    @pl.when(ch > 0)
+    def _():
+        last(second, ch - 1)
+
+    for half in range(2):
+        finish(2, 2, half)
+        z_start(chunks[3 + half])
+    relay(chunks[2])
     complete(chunks[0])
-    project(chunks[2])
+    complete(chunks[1])
     project(chunks[3])
-    relay(chunks[2])
-    complete(chunks[1])
+    project(chunks[4])
     relay(chunks[3])
     complete(chunks[2])
+    relay(chunks[4])
     complete(chunks[3])
+    complete(chunks[4])
 
     for k in range(sent[0]):
         remote(kv.at[0], kv.at[0], kv_send.at[k], kv_recv.at[0], seq=sib).wait_send()
@@ -463,8 +493,8 @@
             pltpu.VMEM((32, 512, HEAD), bf),
             pltpu.VMEM((2, 512, HEAD), bf),
             pltpu.VMEM((2, HEADS, KEYS, ROWS), f32),
-            pltpu.VMEM((2, HEAD + 16, WIDE), f32),
-            pltpu.VMEM((2, 8, WIDE), f32),
+            pltpu.VMEM((3, HEAD + 16, WIDE), f32),
+            pltpu.VMEM((3, 8, WIDE), f32),
             pltpu.VMEM((3, 2, ROWS, COLS), bf),
             pltpu.VMEM((COLS, 4 * COLS), bf),
             pltpu.VMEM((COLS, 4 * COLS), bf),
@@ -472,8 +502,8 @@
             pltpu.VMEM((3, 3, ROWS, COLS), bf),
             pltpu.VMEM((3, 3, ROWS, COLS), bf),
             pltpu.VMEM((3, ROWS, COLS), bf),
-            dma((8,)), dma((4,)), dma((31,)), dma((32,)), dma((3,)), dma((3,)),
-            dma((4,)), dma((4,)), dma((12,)), dma((12,)),
+            dma((8,)), dma((5,)), dma((31,)), dma((32,)), dma((3,)), dma((3,)),
+            dma((5,)), dma((5,)), dma((15,)), dma((15,)),
         ],
         compiler_params=pltpu.CompilerParams(
             collective_id=0, has_side_effects=True, vmem_limit_bytes=VMEM_LIMIT

time: 92.2 us -> 90.5 us (0.982)
  Pallas kernels: 87.7 us -> 86 us
    pallas_call x1, Pallas kernels: 87.7 us -> 86 us  [per_device(): pl.pallas_call(kernel, out_shape=(jax.ShapeDtypeStruct((ROWS, COLS), bf),...]
where the time goes in v3:
time: 90.5 us; the launch traced here: 90.3 us
  Pallas kernels  86 us (95%)
  local copies, waits for them, and re-layouts  3.7 us (4%)
    pallas_call x1, Pallas kernels, per_device(): pl.pallas_call(kernel, out_shape=(jax.ShapeDtypeStruct((ROWS, COLS), bf),...  86 us
    unnamed x2, local copies, waits for them, and re-layouts  3.7 us

profile of v3, /device:TPU:216, one launch (start us, length us, event | category | flops | bytes accessed | tf_op | source)
XLA Modules:
  0.0 90.3 jit_solution(1096481017218911466)
XLA Ops:
  0.6 86.0 %shard_map.95 = (bf16[256,640]{1,0:T(8,128)(2,1)}, bf16[2,256,640]{2,1,0:T(8,128)(2,1)}) custom-call(bf16[256,640]{1,0:T(8,128)(2,1)} %sol_q_in.1, bf16[256,128]{1,0:T(8,128)(2,1)} %sol_k_in.1, bf16[256,128]{1,0:T(8,128)(2,1)} %sol_v_in.1, bf16[2,256,640]{2,1,0:T(8,128)(2,1)} %crit_q_in.1, bf16[2,256,128]{2,1,0:T(8,128)(2,1)} %crit_k_in.1, ...), custom_call_target="tpu_custom_call" | custom-call | flops 20000000000 | bytes 16000000 | tf_op jit(solution)/shard_map/pallas_call | solution.py:478
  86.6 1.7 %copy.12 = bf16[256,640]{1,0:T(8,128)(2,1)} copy(bf16[256,640]{1,0:T(8,128)(2,1)} %get-tuple-element.4) | data formatting | bytes 655360
  88.4 2.0 %copy.13 = bf16[2,256,640]{2,1,0:T(8,128)(2,1)} copy(bf16[2,256,640]{2,1,0:T(8,128)(2,1)} %get-tuple-element.5) | data formatting | bytes 1310720
